TPU v7x, 32 devices: a whole 2x2x4 slice. The times are simulated.
32 devices in a mesh: replica: 8 (over y, x, core), fsdp: 4 (over z).
Axes of the slice: x: 2, y: 2, z: 4, core: 2. Of those that a mesh axis runs over, the one named last changes fastest.
Arguments:
- local_weight: bfloat16 [8, 64, 8192], P('replica', None, 'fsdp'), may hold values from -1 to 1
- anchor: float32 [64, 8192], P(None, 'fsdp'), may hold values from -0.75 to 0.75
- momentum: float32 [64, 8192], P('replica', 'fsdp'), may hold values from -0.3 to 0.3
- tokens: bfloat16 [4096, 64], P(('replica', 'fsdp')), may hold values from -6 to 6
Outputs:
- blended_weight: bfloat16 [8, 64, 8192], P('replica', None, 'fsdp')
- anchor_out: float32 [64, 8192], P(None, 'fsdp')
- momentum_out: float32 [64, 8192], P('replica', 'fsdp')
- product_out: bfloat16 [4096, 8192], P(('replica', 'fsdp'))
All inputs are finite; a program needn't handle non-finite values.
Results may differ from a plain program's by a relative error of at most 0.0051.
Values may be sent and summed in bfloat16 or wider, within the bound.
A program may use at most 64 MiB of HBM per device.

v0:
```python
import jax
import jax.numpy as jnp
from jax import lax
from jax.sharding import PartitionSpec as P

outer_rate = 0.7
decay_rate = 0.9
blend_rate = 0.5


def per_device(local_weight, anchor, momentum, tokens):
    workers = lax.axis_size("replica")
    own_weight = local_weight[0]
    pseudo = (anchor - own_weight.astype(jnp.float32)).astype(jnp.bfloat16)
    pseudo = lax.optimization_barrier(pseudo)
    summed = lax.psum_scatter(
        pseudo.astype(jnp.float32), "replica", scatter_dimension=0, tiled=True
    )
    average = summed / workers
    row_count = summed.shape[0]
    offset = lax.axis_index("replica") * row_count
    anchor_slice = lax.dynamic_slice_in_dim(anchor, offset, row_count, 0)
    momentum_out = decay_rate * momentum + average
    new_slice = anchor_slice - outer_rate * (average + decay_rate * momentum_out)
    anchor_out = lax.all_gather(new_slice, "replica", axis=0, tiled=True)
    blended = (
        blend_rate * anchor_out + (1.0 - blend_rate) * own_weight.astype(jnp.float32)
    ).astype(jnp.bfloat16)
    product_out = jnp.dot(
        tokens,
        lax.all_gather(blended, "fsdp", axis=1, tiled=True),
        preferred_element_type=jnp.float32,
    ).astype(jnp.bfloat16)
    return (blended[None], anchor_out, momentum_out, product_out)


def solution(mesh):
    placed = (
        P("replica", None, "fsdp"),
        P(None, "fsdp"),
        P("replica", "fsdp"),
        P(("replica", "fsdp"), None),
    )
    return jax.shard_map(
        per_device,
        mesh=mesh,
        in_specs=placed,
        out_specs=(
            P("replica", None, "fsdp"),
            P(None, "fsdp"),
            P("replica", "fsdp"),
            P(("replica", "fsdp"), None),
        ),
        check_vma=False,
    )
```

profile of v0, /device:TPU:0, one launch (start us, length us, event | category | flops | bytes accessed | tf_op | source)
XLA Modules:
  0.0 101.3 jit_solution(700612742353672625)
XLA Ops:
  7.2 0.0 copy-start
  7.2 0.0 copy-start.1
  7.2 0.0 copy-start.2
  7.2 0.0 reduce-scatter.2.cloned.1.call-start
  7.2 1.2 %fusion.1 = bf16[64,2048]{1,0:T(8,128)(2,1)S(1)} fusion(f32[64,2048]{1,0:T(8,128)} %param.5, bf16[1,64,2048]{2,1,0:T(8,128)(2,1)} %param.4), kind=kLoop, calls=%fused_computation.4 | loop fusion | flops 393216 | bytes 1048576 | tf_op jit(solution)/shard_map/convert_element_type | solution.py:14
  8.4 0.8 convert_element_type.25
  9.3 0.0 reduce-scatter.2.cloned.1.call-update
  9.3 0.0 all-gather.2.cloned.1.call-start
  9.4 39.2 %reduce-scatter.2.cloned.1.call-done = f32[8,2048]{1,0:T(8,128)} async-done(((f32[64,2048]{1,0:T(8,128)}), f32[8,2048]{1,0:T(8,128)}) %reduce-scatter.2.cloned.1.call-update) | async-done | bytes 65552 | tf_op jit(solution)/shard_map/reduce_scatter | solution.py:16
  48.5 0.0 copy-done.2
  48.5 1.5 %multiply_subtract_fusion = (f32[8,2048]{1,0:T(8,128)S(1)}, f32[8,2048]{1,0:T(8,128)}) fusion(f32[64,2048]{1,0:T(8,128)} %param.5, s32[]{:T(128)S(6)} %select_n.3, f32[8,2048]{1,0:T(8,128)} %reduce-scatter.2.cloned.1.call-done, f32[8,2048]{1,0:T(8,128)S(1)} %copy-done.2), kind=kLoop, calls=%fused_computation.7 | loop fusion | flops 114688 | bytes 327684 | tf_op jit(solution)/shard_map/sub | solution.py:24
  50.0 9.8 %all_gather.6 = f32[64,2048]{1,0:T(8,128)S(1)} all-gather(f32[8,2048]{1,0:T(8,128)S(1)} %get-tuple-element.8), channel_id=1, replica_groups=mesh['replica'=8,'fsdp'=4] {'replica'}, dimensions={0}, use_global_device_ids=true | all-gather | bytes 589824 | tf_op jit(solution)/shard_map/all_gather | solution.py:25
  59.8 0.0 copy-done.1
  59.8 0.8 fusion.3
  60.6 0.0 all-gather.2.cloned.1.call-update
  60.6 28.1 %all-gather.2.cloned.1.call-done = bf16[64,8192]{1,0:T(8,128)(2,1)} async-done(((bf16[64,2048]{1,0:T(8,128)(2,1)}), bf16[64,8192]{1,0:T(8,128)(2,1)}) %all-gather.2.cloned.1.call-update) | async-done | bytes 1048592 | tf_op jit(solution)/shard_map/all_gather | solution.py:31
  88.7 0.0 copy-done
  88.7 2.0 %fusion = bf16[128,8192]{0,1:T(8,128)(2,1)S(1)} fusion(bf16[64,8192]{1,0:T(8,128)(2,1)} %all-gather.2.cloned.1.call-done, bf16[128,64]{0,1:T(8,128)(2,1)S(1)} %copy-done), kind=kOutput, calls=%fused_computation.1 | convolution fusion | flops 135266304 | bytes 3162112 | tf_op jit(solution)/shard_map/dot_general | solution.py:29
  90.7 2.9 %copy.8 = bf16[128,8192]{1,0:T(8,128)(2,1)} copy(bf16[128,8192]{0,1:T(8,128)(2,1)S(1)} %fusion) | data formatting | bytes 4194304
  93.6 0.8 copy.10
Async XLA Ops:
  7.2 81.6 %copy-start = (bf16[128,64]{0,1:T(8,128)(2,1)S(1)}, bf16[128,64]{0,1:T(8,128)(2,1)}, u32[]{:S(2)}) copy-start(bf16[128,64]{0,1:T(8,128)(2,1)} %param.7) | copy-start | bytes 49156
  7.2 52.6 %copy-start.1 = (bf16[1,64,2048]{2,1,0:T(8,128)(2,1)S(1)}, bf16[1,64,2048]{2,1,0:T(8,128)(2,1)}, u32[]{:S(2)}) copy-start(bf16[1,64,2048]{2,1,0:T(8,128)(2,1)} %param.4) | copy-start | bytes 786436
  7.2 41.3 %copy-start.2 = (f32[8,2048]{1,0:T(8,128)S(1)}, f32[8,2048]{1,0:T(8,128)}, u32[]{:S(2)}) copy-start(f32[8,2048]{1,0:T(8,128)} %param.6) | copy-start | bytes 196612
  7.2 41.3 %reduce-scatter.2.cloned.1.call-start = ((), (), s32[]{:S(2)}) async-start(), calls=%async_computation.1 | async-start | bytes 589824 | tf_op jit(solution)/shard_map/reduce_scatter | solution.py:16
  9.3 79.4 %all-gather.2.cloned.1.call-start = ((), (), s32[]{:S(2)}) async-start(), calls=%async_computation.2 | async-start | bytes 1310720 | tf_op jit(solution)/shard_map/all_gather | solution.py:31
Sparse Core Ops, SparseCore 0:
  11.7 36.7 reduce-scatter.1
  60.7 27.9 all-gather.1
where the time goes:
time: 102 us; the launch traced here: 101 us
  waiting for transfers between devices  67.3 us (66%)
  between operations  14.1 us (14%)
  blocking collectives  9.78 us (10%)
  other arithmetic  4.31 us (4%)
  local copies, waits for them, and re-layouts  3.7 us (4%)
  matrix products  1.99 us (2%)
    reduce_scatter x1, waiting for transfers between devices, per_device(): lax.psum_scatter(pseudo.astype(jnp.float32), 'replica', scatter_dimension...  39.2 us
    all_gather x1, waiting for transfers between devices, per_device(): lax.all_gather(blended, 'fsdp', axis=1, tiled=True)  28.1 us
    all_gather x1, blocking collectives, per_device(): anchor_out = lax.all_gather(new_slice, 'replica', axis=0, tiled=True)  9.78 us
    unnamed x8, local copies, waits for them, and re-layouts  3.7 us
  transfers between devices with their start and end apart: 2, of which 2 were waited for; matrix products, arithmetic and copies ran while one was open for 0% of the time, Pallas kernels for 0%

commit v1 on v0

v1 whole, which is shorter than its diff:
```python
import functools

import jax
import jax.numpy as jnp
from jax import lax
from jax.experimental import pallas as pl
from jax.experimental.pallas import tpu as pltpu
from jax.sharding import PartitionSpec as P

outer_rate = 0.7
decay_rate = 0.9
blend_rate = 0.5
MESH = pl.DeviceIdType.MESH


def kernel(
    n_r, n_f, chunks, fold,
    lw_ref, anchor_ref, mom_ref, tok_ref,
    blend_ref, aout_ref, mout_ref, prod_ref,
    rs_send, rs_recv, gath,
    rs_ssem, rs_rsem, ag_ssem, ag_rsem, z_ssem, z_rsem,
):
    r = lax.axis_index("replica")
    f = lax.axis_index("fsdp")
    frag, cols = anchor_ref.shape
    rows = frag // n_r
    w = cols // chunks
    half = w // fold

    barrier = pltpu.get_barrier_semaphore()

    def greet(i, _):
        pl.semaphore_signal(
            barrier, inc=1, device_id=(lax.rem(r + i, n_r), f), device_id_type=MESH
        )
        return 0

    lax.fori_loop(1, n_r, greet, 0)

    @pl.when(f > 0)
    def _():
        pl.semaphore_signal(barrier, inc=1, device_id=(r, f - 1), device_id_type=MESH)

    @pl.when(f < n_f - 1)
    def _():
        pl.semaphore_signal(barrier, inc=1, device_id=(r, f + 1), device_id_type=MESH)

    for c in range(chunks):
        for j in range(n_r):
            part = (
                anchor_ref[j * rows : (j + 1) * rows, c * w : (c + 1) * w]
                - lw_ref[0, j * rows : (j + 1) * rows, c * w : (c + 1) * w].astype(jnp.float32)
            )
            part = jnp.concatenate(
                [part[:, k * half : (k + 1) * half] for k in range(fold)], axis=0
            )
            rs_send[c, j] = part.astype(jnp.bfloat16)

    left = (f + n_f - 1) // n_f
    right = (2 * n_f - 2 - f) // n_f
    pl.semaphore_wait(barrier, n_r - 1 + left + right)

    def rs_copy(c, peer, slot):
        return pltpu.make_async_remote_copy(
            src_ref=rs_send.at[c, peer],
            dst_ref=rs_recv.at[c, slot],
            send_sem=rs_ssem.at[c, peer],
            recv_sem=rs_rsem.at[c, slot],
            device_id=(peer, f),
            device_id_type=MESH,
        )

    def ag_copy(c, peer, owner):
        block = aout_ref.at[
            pl.ds(pl.multiple_of(owner * rows, rows), rows), pl.ds(c * w, w)
        ]
        return pltpu.make_async_remote_copy(
            src_ref=block,
            dst_ref=block,
            send_sem=ag_ssem.at[c, peer],
            recv_sem=ag_rsem.at[c, owner],
            device_id=(peer, f),
            device_id_type=MESH,
        )

    def z_copy(c, block, side):
        return pltpu.make_async_remote_copy(
            src_ref=gath.at[block, c],
            dst_ref=gath.at[block, c],
            send_sem=z_ssem.at[c, block, side],
            recv_sem=z_rsem.at[c, block],
            device_id=(r, f + 1 if side == 0 else f - 1),
            device_id_type=MESH,
        )

    def each_peer(body):
        def step(i, _):
            body(lax.rem(r + i, n_r))
            return 0

        lax.fori_loop(1, n_r, step, 0)

    for c in range(chunks):
        each_peer(lambda peer: rs_copy(c, peer, r).start())

    own = pl.ds(pl.multiple_of(r * rows, rows), rows)
    for c in range(chunks):
        at = slice(c * w, (c + 1) * w)

        def arrived(i, total):
            peer = lax.rem(r + i, n_r)
            rs_copy(c, peer, peer).wait_recv()
            return total + rs_recv[c, peer].astype(jnp.float32)

        total = lax.fori_loop(1, n_r, arrived, rs_send[c, r].astype(jnp.float32))
        total = jnp.concatenate(
            [total[k * rows : (k + 1) * rows] for k in range(fold)], axis=1
        )
        average = total / n_r
        mom = decay_rate * mom_ref[:, at] + average
        mout_ref[:, at] = mom
        aout_ref[own, at] = anchor_ref[own, at] - outer_rate * (average + decay_rate * mom)
        each_peer(lambda peer: ag_copy(c, peer, r).start())

    def multiply(c, block):
        prod_ref[:, pl.ds(pl.multiple_of(block * cols + c * w, w), w)] = jnp.dot(
            tok_ref[...], gath[block, c], preferred_element_type=jnp.float32
        ).astype(jnp.bfloat16)

    for c in range(chunks):
        at = slice(c * w, (c + 1) * w)
        each_peer(lambda peer: ag_copy(c, peer, peer).wait_recv())
        blended = (
            blend_rate * aout_ref[:, at]
            + (1.0 - blend_rate) * lw_ref[0, :, at].astype(jnp.float32)
        ).astype(jnp.bfloat16)
        gath[f, c] = blended

        @pl.when(f < n_f - 1)
        def _():
            z_copy(c, f, 0).start()

        @pl.when(f > 0)
        def _():
            z_copy(c, f, 1).start()

        blend_ref[0, :, at] = blended
        multiply(c, f)

    for k in range(1, n_f):
        for c in range(chunks):

            @pl.when(f - k >= 0)
            def _():
                z_copy(c, f - k, 0).wait_recv()

                @pl.when(f < n_f - 1)
                def _():
                    z_copy(c, f - k, 0).start()

            @pl.when(f + k < n_f)
            def _():
                z_copy(c, f + k, 1).wait_recv()

                @pl.when(f > 0)
                def _():
                    z_copy(c, f + k, 1).start()

            @pl.when(f - k >= 0)
            def _():
                multiply(c, f - k)

            @pl.when(f + k < n_f)
            def _():
                multiply(c, f + k)

    for c in range(chunks):

        def sent(peer):
            rs_copy(c, peer, r).wait_send()
            ag_copy(c, peer, r).wait_send()

        each_peer(sent)
        for k in range(n_f):

            @pl.when((f - k >= 0) & (f < n_f - 1))
            def _():
                z_copy(c, f - k, 0).wait_send()

            @pl.when((f + k < n_f) & (f > 0))
            def _():
                z_copy(c, f + k, 1).wait_send()


def per_device(local_weight, anchor, momentum, tokens):
    n_r, n_f = lax.axis_size("replica"), lax.axis_size("fsdp")
    frag, cols = anchor.shape
    rows = frag // n_r
    fold = 1 if rows % 16 == 0 else 2
    chunks = max(1, min(4, cols // (128 * fold)))
    w = cols // chunks
    count = tokens.shape[0]
    vmem = pl.BlockSpec(memory_space=pltpu.VMEM)
    return pl.pallas_call(
        functools.partial(kernel, n_r, n_f, chunks, fold),
        out_shape=(
            jax.ShapeDtypeStruct(local_weight.shape, jnp.bfloat16),
            jax.ShapeDtypeStruct(anchor.shape, jnp.float32),
            jax.ShapeDtypeStruct(momentum.shape, jnp.float32),
            jax.ShapeDtypeStruct((count, cols * n_f), jnp.bfloat16),
        ),
        in_specs=[vmem] * 4,
        out_specs=[vmem] * 4,
        scratch_shapes=[
            pltpu.VMEM((chunks, n_r, rows * fold, w // fold), jnp.bfloat16),
            pltpu.VMEM((chunks, n_r, rows * fold, w // fold), jnp.bfloat16),
            pltpu.VMEM((n_f, chunks, frag, w), jnp.bfloat16),
            pltpu.SemaphoreType.DMA((chunks, n_r)),
            pltpu.SemaphoreType.DMA((chunks, n_r)),
            pltpu.SemaphoreType.DMA((chunks, n_r)),
            pltpu.SemaphoreType.DMA((chunks, n_r)),
            pltpu.SemaphoreType.DMA((chunks, n_f, 2)),
            pltpu.SemaphoreType.DMA((chunks, n_f)),
        ],
        compiler_params=pltpu.CompilerParams(
            collective_id=0, has_side_effects=True, vmem_limit_bytes=40 * 2**20
        ),
        cost_estimate=pl.CostEstimate(
            flops=2 * count * frag * cols * n_f,
            bytes_accessed=4 * frag * cols * 3 + 2 * count * cols * n_f,
            transcendentals=0,
        ),
    )(local_weight, anchor, momentum, tokens)


def solution(mesh):
    placed = (
        P("replica", None, "fsdp"),
        P(None, "fsdp"),
        P("replica", "fsdp"),
        P(("replica", "fsdp"), None),
    )
    return jax.shard_map(
        per_device,
        mesh=mesh,
        in_specs=placed,
        out_specs=placed,
        check_vma=False,
    )
```

time: 102 us -> 40.9 us (0.40)
  waiting for transfers between devices: 67.3 us -> 0 us
  Pallas kernels: 0 us -> 32.9 us
  between operations: 14.1 us -> 0.65 us
  blocking collectives: 9.78 us -> 0 us
  other arithmetic: 4.31 us -> 0 us
  local copies, waits for them, and re-layouts: 3.7 us -> 7.1 us
  matrix products: 1.99 us -> 0 us
    reduce_scatter x1 -> x0, waiting for transfers between devices: 39.2 us -> none  [per_device(): lax.psum_scatter(pseudo.astype(jnp.float32), 'replica', scatter_dimension...]
    pallas_call x0 -> x1, Pallas kernels: none -> 32.9 us  [per_device(): pl.pallas_call(functools.partial(kernel, n_r, n_f, chunks, fold), out_sha...]
    all_gather x1 -> x0, waiting for transfers between devices: 28.1 us -> none  [per_device(): lax.all_gather(blended, 'fsdp', axis=1, tiled=True)]
    all_gather x1 -> x0, blocking collectives: 9.78 us -> none  [per_device(): anchor_out = lax.all_gather(new_slice, 'replica', axis=0, tiled=True)]
    unnamed x8 -> x11, local copies, waits for them, and re-layouts: 3.7 us -> 7.1 us
    convert_element_type x3 -> x0, other arithmetic: 2.8 us -> none  [the longest x1 1.19 us: per_device(): pseudo = (anchor - own_weight.astype(jnp.float32)).astype(jnp.bfloat16)]
    dot_general x1 -> x0, matrix products: 1.99 us -> none  [per_device(): jnp.dot(tokens, lax.all_gather(blended, 'fsdp', axis=1, tiled=True), pref...]
    sub x1 -> x0, other arithmetic: 1.52 us -> none  [per_device(): anchor_slice - outer_rate * (average + decay_rate * momentum_out)]
  transfers between devices with their start and end apart: 2 -> 0, of which waited for: 2 -> 0; matrix products, arithmetic and copies ran while one was open for 0% -> 0% of each run, Pallas kernels for 0% -> 0%
where the time goes in v1:
time: 40.9 us; the launch traced here: 40.6 us
  Pallas kernels  32.9 us (80%)
  local copies, waits for them, and re-layouts  7.1 us (17%)
  between operations  0.65 us (2%)
    pallas_call x1, Pallas kernels, per_device(): pl.pallas_call(functools.partial(kernel, n_r, n_f, chunks, fold), out_sha...  32.9 us
    unnamed x11, local copies, waits for them, and re-layouts  7.1 us

profile of v1, /device:TPU:0, one launch (start us, length us, event | category | flops | bytes accessed | tf_op | source)
XLA Modules:
  0.0 40.6 jit_solution(3378878808643838242)
XLA Ops:
  0.6 0.8 %copy.8.tok_ref = bf16[128,64]{1,0:T(8,128)(2,1)S(1)} copy(bf16[128,64]{0,1:T(8,128)(2,1)} %param.7) | data formatting | bytes 32768 | tf_op args[3]
  1.5 0.0 copy-start
  1.5 1.0 %copy-done = f32[64,2048]{1,0:T(8,128)S(1)} copy-done((f32[64,2048]{1,0:T(8,128)S(1)}, f32[64,2048]{1,0:T(8,128)}, u32[]{:S(2)}) %copy-start) | copy-done | bytes 524312
  2.5 0.0 copy-start.1
  2.5 0.9 %copy-done.1 = bf16[1,64,2048]{2,1,0:T(8,128)(2,1)S(1)} copy-done((bf16[1,64,2048]{2,1,0:T(8,128)(2,1)S(1)}, bf16[1,64,2048]{2,1,0:T(8,128)(2,1)}, u32[]{:S(2)}) %copy-start.1) | copy-done | bytes 262168
  3.5 0.0 copy-start.2
  3.5 0.8 %copy-done.2 = f32[8,2048]{1,0:T(8,128)S(1)} copy-done((f32[8,2048]{1,0:T(8,128)S(1)}, f32[8,2048]{1,0:T(8,128)}, u32[]{:S(2)}) %copy-start.2) | copy-done | bytes 65560
  4.3 32.9 %shard_map.75 = (bf16[1,64,2048]{2,1,0:T(8,128)(2,1)S(1)}, f32[64,2048]{1,0:T(8,128)S(1)}, f32[8,2048]{1,0:T(8,128)S(1)}, bf16[128,8192]{1,0:T(8,128)(2,1)S(1)}) custom-call(bf16[1,64,2048]{2,1,0:T(8,128)(2,1)S(1)} %copy-done.1, f32[64,2048]{1,0:T(8,128)S(1)} %copy-done, f32[8,2048]{1,0:T(8,128)S(1)} %copy-done.2, bf16[128,64]{1,0:T(8,128)(2,1)S(1)} %copy.8.tok_ref), custom_call_target="tpu_custom_call" | custom-call | flops 134217728 | bytes 3670016 | tf_op jit(solution)/shard_map/pallas_call | solution.py:204
  37.2 0.7 %copy.13 = bf16[1,64,2048]{2,1,0:T(8,128)(2,1)} copy(bf16[1,64,2048]{2,1,0:T(8,128)(2,1)S(1)} %get-tuple-element.8) | data formatting | bytes 524288
  37.9 0.8 %copy.14 = f32[64,2048]{1,0:T(8,128)} copy(f32[64,2048]{1,0:T(8,128)S(1)} %get-tuple-element.9) | data formatting | bytes 1048576
  38.7 0.6 %copy.15 = f32[8,2048]{1,0:T(8,128)} copy(f32[8,2048]{1,0:T(8,128)S(1)} %get-tuple-element.10) | data formatting | bytes 131072
  39.3 1.3 %copy.16 = bf16[128,8192]{1,0:T(8,128)(2,1)} copy(bf16[128,8192]{1,0:T(8,128)(2,1)S(1)} %get-tuple-element.11) | data formatting | bytes 4194304
Async XLA Ops:
  1.5 1.1 %copy-start = (f32[64,2048]{1,0:T(8,128)S(1)}, f32[64,2048]{1,0:T(8,128)}, u32[]{:S(2)}) copy-start(f32[64,2048]{1,0:T(8,128)} %anchor_ref.1) | copy-start | bytes 1572868
  2.5 0.9 %copy-start.1 = (bf16[1,64,2048]{2,1,0:T(8,128)(2,1)S(1)}, bf16[1,64,2048]{2,1,0:T(8,128)(2,1)}, u32[]{:S(2)}) copy-start(bf16[1,64,2048]{2,1,0:T(8,128)(2,1)} %lw_ref.1) | copy-start | bytes 786436
  3.5 0.8 %copy-start.2 = (f32[8,2048]{1,0:T(8,128)S(1)}, f32[8,2048]{1,0:T(8,128)}, u32[]{:S(2)}) copy-start(f32[8,2048]{1,0:T(8,128)} %mom_ref.1) | copy-start | bytes 196612

commit v2 on v1

--- a/solution.py
+++ b/solution.py
@@ -15,13 +15,22 @@
 
 def kernel(
     n_r, n_f, chunks, fold,
-    lw_ref, anchor_ref, mom_ref, tok_ref,
+    lw_hbm, anchor_hbm, mom_hbm, tok_hbm,
     blend_ref, aout_ref, mout_ref, prod_ref,
-    rs_send, rs_recv, gath,
+    lw_ref, anchor_ref, mom_ref, tok_ref, rs_send, rs_recv, gath, in_sem,
     rs_ssem, rs_rsem, ag_ssem, ag_rsem, z_ssem, z_rsem,
 ):
     r = lax.axis_index("replica")
     f = lax.axis_index("fsdp")
+    fetches = [
+        pltpu.make_async_copy(source, target, in_sem.at[i])
+        for i, (source, target) in enumerate((
+            (lw_hbm, lw_ref), (anchor_hbm, anchor_ref),
+            (mom_hbm, mom_ref), (tok_hbm, tok_ref),
+        ))
+    ]
+    for fetch in fetches:
+        fetch.start()
     frag, cols = anchor_ref.shape
     rows = frag // n_r
     w = cols // chunks
@@ -44,6 +53,9 @@
     @pl.when(f < n_f - 1)
     def _():
         pl.semaphore_signal(barrier, inc=1, device_id=(r, f + 1), device_id_type=MESH)
+
+    fetches[0].wait()
+    fetches[1].wait()
 
     for c in range(chunks):
         for j in range(n_r):
@@ -103,6 +115,8 @@
     for c in range(chunks):
         each_peer(lambda peer: rs_copy(c, peer, r).start())
 
+    fetches[2].wait()
+    fetches[3].wait()
     own = pl.ds(pl.multiple_of(r * rows, rows), rows)
     for c in range(chunks):
         at = slice(c * w, (c + 1) * w)
@@ -123,8 +137,11 @@
         each_peer(lambda peer: ag_copy(c, peer, r).start())
 
     def multiply(c, block):
-        prod_ref[:, pl.ds(pl.multiple_of(block * cols + c * w, w), w)] = jnp.dot(
-            tok_ref[...], gath[block, c], preferred_element_type=jnp.float32
+        prod_ref[:, pl.ds(pl.multiple_of(block * cols + c * w, w), w)] = lax.dot_general(
+            tok_ref[...],
+            gath[block, c],
+            (((0,), (0,)), ((), ())),
+            preferred_element_type=jnp.float32,
         ).astype(jnp.bfloat16)
 
     for c in range(chunks):
@@ -190,6 +207,18 @@
             @pl.when((f + k < n_f) & (f > 0))
             def _():
                 z_copy(c, f + k, 1).wait_send()
+
+
+def write_out(*refs):
+    count = (len(refs) - 1) // 2
+    copies = [
+        pltpu.make_async_copy(refs[i], refs[count + i], refs[-1].at[i])
+        for i in range(count)
+    ]
+    for copy in copies:
+        copy.start()
+    for copy in copies:
+        copy.wait()
 
 
 def per_device(local_weight, anchor, momentum, tokens):
@@ -200,8 +229,9 @@
     chunks = max(1, min(4, cols // (128 * fold)))
     w = cols // chunks
     count = tokens.shape[0]
+    hbm = pl.BlockSpec(memory_space=pltpu.HBM)
     vmem = pl.BlockSpec(memory_space=pltpu.VMEM)
-    return pl.pallas_call(
+    results = pl.pallas_call(
         functools.partial(kernel, n_r, n_f, chunks, fold),
         out_shape=(
             jax.ShapeDtypeStruct(local_weight.shape, jnp.bfloat16),
@@ -209,12 +239,17 @@
             jax.ShapeDtypeStruct(momentum.shape, jnp.float32),
             jax.ShapeDtypeStruct((count, cols * n_f), jnp.bfloat16),
         ),
-        in_specs=[vmem] * 4,
+        in_specs=[hbm] * 4,
         out_specs=[vmem] * 4,
         scratch_shapes=[
+            pltpu.VMEM(local_weight.shape, jnp.bfloat16),
+            pltpu.VMEM(anchor.shape, jnp.float32),
+            pltpu.VMEM(momentum.shape, jnp.float32),
+            pltpu.VMEM(tokens.shape[::-1], jnp.bfloat16),
             pltpu.VMEM((chunks, n_r, rows * fold, w // fold), jnp.bfloat16),
             pltpu.VMEM((chunks, n_r, rows * fold, w // fold), jnp.bfloat16),
             pltpu.VMEM((n_f, chunks, frag, w), jnp.bfloat16),
+            pltpu.SemaphoreType.DMA((4,)),
             pltpu.SemaphoreType.DMA((chunks, n_r)),
             pltpu.SemaphoreType.DMA((chunks, n_r)),
             pltpu.SemaphoreType.DMA((chunks, n_r)),
@@ -230,7 +265,18 @@
             bytes_accessed=4 * frag * cols * 3 + 2 * count * cols * n_f,
             transcendentals=0,
         ),
-    )(local_weight, anchor, momentum, tokens)
+    )(*(
+        pltpu.with_memory_space_constraint(x, pltpu.HBM)
+        for x in (local_weight, anchor, momentum, tokens.T)
+    ))
+    return pl.pallas_call(
+        write_out,
+        out_shape=[jax.ShapeDtypeStruct(x.shape, x.dtype) for x in results],
+        in_specs=[vmem] * 4,
+        out_specs=[hbm] * 4,
+        scratch_shapes=[pltpu.SemaphoreType.DMA((4,))],
+        compiler_params=pltpu.CompilerParams(vmem_limit_bytes=16 * 2**20),
+    )(*results)
 
 
 def solution(mesh):

time: 40.9 us -> 35.4 us (0.87)
  local copies, waits for them, and re-layouts: 7.1 us -> 0 us
  Pallas kernels: 32.9 us -> 34.6 us
    unnamed x11 -> x0, local copies, waits for them, and re-layouts: 7.1 us -> none
    pallas_call x0 -> x1, Pallas kernels: none -> 1.64 us  [per_device(): pl.pallas_call(write_out, out_shape=[jax.ShapeDtypeStruct(x.shape, x.dtyp...]
where the time goes in v2:
time: 35.4 us; the launch traced here: 35.3 us
  Pallas kernels  34.6 us (98%)
  between operations  0.64 us (2%)
    pallas_call x1, Pallas kernels, per_device(): pl.pallas_call(functools.partial(kernel, n_r, n_f, chunks, fold), out_sha...  33 us
    pallas_call x1, Pallas kernels, per_device(): pl.pallas_call(write_out, out_shape=[jax.ShapeDtypeStruct(x.shape, x.dtyp...  1.64 us

profile of v2, /device:TPU:0, one launch (start us, length us, event | category | flops | bytes accessed | tf_op | source)
XLA Modules:
  0.0 35.3 jit_solution(8759317367733778252)
XLA Ops:
  0.6 33.0 %shard_map.75 = (bf16[1,64,2048]{2,1,0:T(8,128)(2,1)S(1)}, f32[64,2048]{1,0:T(8,128)S(1)}, f32[8,2048]{1,0:T(8,128)S(1)}, bf16[128,8192]{1,0:T(8,128)(2,1)S(1)}) custom-call(bf16[1,64,2048]{2,1,0:T(8,128)(2,1)} %lw_hbm.1, f32[64,2048]{1,0:T(8,128)} %anchor_hbm.1, f32[8,2048]{1,0:T(8,128)} %mom_hbm.1, bf16[64,128]{1,0:T(8,128)(2,1)} %bitcast.1), custom_call_target="tpu_custom_call" | custom-call | flops 134217728 | bytes 3670016 | tf_op jit(solution)/shard_map/pallas_call | solution.py:234
  33.7 1.6 %shard_map.76 = (bf16[1,64,2048]{2,1,0:T(8,128)(2,1)}, f32[64,2048]{1,0:T(8,128)}, f32[8,2048]{1,0:T(8,128)}, bf16[128,8192]{1,0:T(8,128)(2,1)}) custom-call(bf16[1,64,2048]{2,1,0:T(8,128)(2,1)S(1)} %get-tuple-element.8.refs_0_, f32[64,2048]{1,0:T(8,128)S(1)} %get-tuple-element.9.refs_1_, f32[8,2048]{1,0:T(8,128)S(1)} %get-tuple-element.10.refs_2_, ...), custom_call_target="tpu_custom_call" | custom-call | tf_op jit(solution)/shard_map/pallas_call | solution.py:272

commit v3 on v0

v3 whole, which is shorter than its diff:
```python
import functools

import jax
import jax.numpy as jnp
from jax import lax
from jax.experimental import pallas as pl
from jax.experimental.pallas import tpu as pltpu
from jax.sharding import PartitionSpec as P

outer_rate = 0.7
decay_rate = 0.9
blend_rate = 0.5
MESH = pl.DeviceIdType.MESH


def kernel(
    n_r, n_f, chunks, fold,
    lw_hbm, anchor_hbm, mom_hbm, tok_hbm,
    blend_ref, aout_ref, mout_ref, prod_ref,
    anchor_ref, mom_ref, tok_ref, rs_send, rs_recv, weights, news, in_sem,
    rs_ssem, rs_rsem, ag_ssem, ag_rsem, z_ssem, z_rsem, n_ssem, n_rsem, d_ssem, d_rsem,
):
    r = lax.axis_index("replica")
    f = lax.axis_index("fsdp")
    frag, cols = anchor_ref.shape
    rows = frag // n_r
    w = cols // chunks
    half = cols // fold

    fetches = [
        pltpu.make_async_copy(source, target, in_sem.at[i])
        for i, (source, target) in enumerate(
            [
                (lw_hbm.at[0, :, pl.ds(c * w, w)], weights.at[f, c])
                for c in range(chunks)
            ]
            + [(anchor_hbm, anchor_ref), (mom_hbm, mom_ref), (tok_hbm, tok_ref)]
        )
    ]
    for fetch in fetches:
        fetch.start()

    barrier = pltpu.get_barrier_semaphore()

    def each_peer(body):
        def step(i, _):
            body(lax.rem(r + i, n_r))
            return 0

        lax.fori_loop(1, n_r, step, 0)

    def each_place(body):
        def step(i, _):
            body(lax.rem(f + i, n_f))
            return 0

        lax.fori_loop(1, n_f, step, 0)

    each_peer(
        lambda peer: pl.semaphore_signal(
            barrier, inc=1, device_id=(peer, f), device_id_type=MESH
        )
    )
    each_place(
        lambda place: pl.semaphore_signal(
            barrier, inc=1, device_id=(r, place), device_id_type=MESH
        )
    )
    for fetch in fetches[: chunks + 1]:
        fetch.wait()

    for j in range(n_r):
        at = slice(j * rows, (j + 1) * rows)
        own_rows = jnp.concatenate(
            [weights[f, c].astype(jnp.float32)[at] for c in range(chunks)], axis=1
        )
        part = anchor_ref[at, :] - own_rows
        rs_send[j] = jnp.concatenate(
            [part[:, k * half : (k + 1) * half] for k in range(fold)], axis=0
        ).astype(jnp.bfloat16)

    pl.semaphore_wait(barrier, n_r + n_f - 2)

    def rs_copy(peer, slot):
        return pltpu.make_async_remote_copy(
            src_ref=rs_send.at[peer],
            dst_ref=rs_recv.at[slot],
            send_sem=rs_ssem.at[peer],
            recv_sem=rs_rsem.at[slot],
            device_id=(peer, f),
            device_id_type=MESH,
        )

    def ag_copy(peer, owner):
        block = aout_ref.at[pl.ds(pl.multiple_of(owner * rows, rows), rows), :]
        return pltpu.make_async_remote_copy(
            src_ref=block,
            dst_ref=block,
            send_sem=ag_ssem.at[peer],
            recv_sem=ag_rsem.at[owner],
            device_id=(peer, f),
            device_id_type=MESH,
        )

    def z_copy(c, block, side):
        return pltpu.make_async_remote_copy(
            src_ref=weights.at[block, c],
            dst_ref=weights.at[block, c],
            send_sem=z_ssem.at[c, block, side],
            recv_sem=z_rsem.at[c, block],
            device_id=(r, f + 1 if side == 0 else f - 1),
            device_id_type=MESH,
        )

    def n_copy(place, block):
        return pltpu.make_async_remote_copy(
            src_ref=news.at[block, r],
            dst_ref=news.at[block, r],
            send_sem=n_ssem.at[place],
            recv_sem=n_rsem.at[block],
            device_id=(r, place),
            device_id_type=MESH,
        )

    def d_copy(peer, block, owner):
        return pltpu.make_async_remote_copy(
            src_ref=news.at[block, owner],
            dst_ref=news.at[block, owner],
            send_sem=d_ssem.at[block, peer],
            recv_sem=d_rsem.at[block, owner],
            device_id=(peer, f),
            device_id_type=MESH,
        )

    def send_on(c, block):
        @pl.when((block <= f) & (f < n_f - 1))
        def _():
            z_copy(c, block, 0).start()

        @pl.when((block >= f) & (f > 0))
        def _():
            z_copy(c, block, 1).start()

    def at_distance(k, body):
        @pl.when(f - k >= 0)
        def _():
            body(f - k)

        @pl.when(f + k < n_f)
        def _():
            body(f + k)

    each_peer(lambda peer: rs_copy(peer, r).start())
    for c in range(chunks):
        send_on(c, f)

    fetches[chunks + 1].wait()
    fetches[chunks + 2].wait()
    own = pl.ds(pl.multiple_of(r * rows, rows), rows)

    each_peer(lambda peer: rs_copy(peer, peer).wait_recv())
    rs_recv[r] = rs_send[r]
    total = rs_recv[0].astype(jnp.float32)
    for j in range(1, n_r):
        total = total + rs_recv[j].astype(jnp.float32)
    total = jnp.concatenate(
        [total[k * rows : (k + 1) * rows] for k in range(fold)], axis=1
    )
    average = total / n_r
    mom = decay_rate * mom_ref[...] + average
    mout_ref[...] = mom
    new = anchor_ref[own, :] - outer_rate * (average + decay_rate * mom)
    aout_ref[own, :] = new
    news[f, r] = jnp.concatenate(
        [new[:, k * half : (k + 1) * half] for k in range(fold)], axis=0
    ).astype(jnp.bfloat16)
    each_place(lambda place: n_copy(place, f).start())
    each_peer(lambda peer: ag_copy(peer, r).start())

    def forward(k):
        for c in range(chunks):

            def body(block):
                z_copy(c, block, 0).wait_recv()
                send_on(c, block)

            at_distance(k, body)

    def spread(k):
        def body(block):
            n_copy(block, block).wait_recv()
            each_peer(lambda peer: d_copy(peer, block, r).start())

        at_distance(k, body)

    def multiply(c, block, weight):
        prod_ref[:, pl.ds(pl.multiple_of(block * cols + c * w, w), w)] = lax.dot_general(
            tok_ref[...],
            weight,
            (((0,), (0,)), ((), ())),
            preferred_element_type=jnp.float32,
        ).astype(jnp.bfloat16)

    def blend(new_rows, weight):
        return (
            blend_rate * new_rows + (1.0 - blend_rate) * weight.astype(jnp.float32)
        ).astype(jnp.bfloat16)

    def finish(k):
        at_distance(
            k,
            lambda block: each_peer(lambda peer: d_copy(peer, block, peer).wait_recv()),
        )
        for c in range(chunks):
            part, start = (c * w) // half, (c * w) % half

            def body(block):
                if k == n_f - 1:
                    z_copy(c, block, 0).wait_recv()
                new_rows = news[block, :, :, start : start + w].astype(jnp.float32)
                new_rows = new_rows[:, part * rows : (part + 1) * rows, :]
                multiply(
                    c, block, blend(new_rows.reshape(frag, w), weights[block, c])
                )

            at_distance(k, body)

    spread(1)
    if n_f > 2:
        forward(1)
    for k in range(2, n_f):
        spread(k)
    each_peer(lambda peer: ag_copy(peer, peer).wait_recv())
    for c in range(chunks):
        at = slice(c * w, (c + 1) * w)
        blended = blend(aout_ref[:, at], weights[f, c])
        blend_ref[0, :, at] = blended
        multiply(c, f, blended)
    for k in range(1, n_f):
        if k + 1 < n_f - 1:
            forward(k + 1)
        finish(k)

    def sent(peer):
        rs_copy(peer, r).wait_send()
        ag_copy(peer, r).wait_send()
        each_place(lambda place: d_copy(peer, place, r).wait_send())

    each_peer(sent)
    each_place(lambda place: n_copy(place, f).wait_send())
    for c in range(chunks):
        for k in range(n_f):

            @pl.when((f - k >= 0) & (f < n_f - 1))
            def _():
                z_copy(c, f - k, 0).wait_send()

            @pl.when((f + k < n_f) & (f > 0))
            def _():
                z_copy(c, f + k, 1).wait_send()


def write_out(*refs):
    count = (len(refs) - 1) // 2
    copies = [
        pltpu.make_async_copy(refs[i], refs[count + i], refs[-1].at[i])
        for i in range(count)
    ]
    for copy in copies:
        copy.start()
    for copy in copies:
        copy.wait()


def per_device(local_weight, anchor, momentum, tokens):
    n_r, n_f = lax.axis_size("replica"), lax.axis_size("fsdp")
    frag, cols = anchor.shape
    rows = frag // n_r
    fold = 1 if rows % 16 == 0 else 2
    chunks = max(1, min(4, cols // (128 * fold)))
    w = cols // chunks
    count = tokens.shape[0]
    hbm = pl.BlockSpec(memory_space=pltpu.HBM)
    vmem = pl.BlockSpec(memory_space=pltpu.VMEM)
    results = pl.pallas_call(
        functools.partial(kernel, n_r, n_f, chunks, fold),
        out_shape=(
            jax.ShapeDtypeStruct(local_weight.shape, jnp.bfloat16),
            jax.ShapeDtypeStruct(anchor.shape, jnp.float32),
            jax.ShapeDtypeStruct(momentum.shape, jnp.float32),
            jax.ShapeDtypeStruct((count, cols * n_f), jnp.bfloat16),
        ),
        in_specs=[hbm] * 4,
        out_specs=[vmem] * 4,
        scratch_shapes=[
            pltpu.VMEM(anchor.shape, jnp.float32),
            pltpu.VMEM(momentum.shape, jnp.float32),
            pltpu.VMEM(tokens.shape[::-1], jnp.bfloat16),
            pltpu.VMEM((n_r, rows * fold, cols // fold), jnp.bfloat16),
            pltpu.VMEM((n_r, rows * fold, cols // fold), jnp.bfloat16),
            pltpu.VMEM((n_f, chunks, frag, w), jnp.bfloat16),
            pltpu.VMEM((n_f, n_r, rows * fold, cols // fold), jnp.bfloat16),
            pltpu.SemaphoreType.DMA((chunks + 3,)),
            pltpu.SemaphoreType.DMA((n_r,)),
            pltpu.SemaphoreType.DMA((n_r,)),
            pltpu.SemaphoreType.DMA((n_r,)),
            pltpu.SemaphoreType.DMA((n_r,)),
            pltpu.SemaphoreType.DMA((chunks, n_f, 2)),
            pltpu.SemaphoreType.DMA((chunks, n_f)),
            pltpu.SemaphoreType.DMA((n_f,)),
            pltpu.SemaphoreType.DMA((n_f,)),
            pltpu.SemaphoreType.DMA((n_f, n_r)),
            pltpu.SemaphoreType.DMA((n_f, n_r)),
        ],
        compiler_params=pltpu.CompilerParams(
            collective_id=0, has_side_effects=True, vmem_limit_bytes=40 * 2**20
        ),
        cost_estimate=pl.CostEstimate(
            flops=2 * count * frag * cols * n_f,
            bytes_accessed=4 * frag * cols * 3 + 2 * count * cols * n_f,
            transcendentals=0,
        ),
    )(*(
        pltpu.with_memory_space_constraint(x, pltpu.HBM)
        for x in (local_weight, anchor, momentum, tokens.T)
    ))
    return pl.pallas_call(
        write_out,
        out_shape=[jax.ShapeDtypeStruct(x.shape, x.dtype) for x in results],
        in_specs=[vmem] * 4,
        out_specs=[hbm] * 4,
        scratch_shapes=[pltpu.SemaphoreType.DMA((4,))],
        compiler_params=pltpu.CompilerParams(vmem_limit_bytes=16 * 2**20),
    )(*results)


def solution(mesh):
    placed = (
        P("replica", None, "fsdp"),
        P(None, "fsdp"),
        P("replica", "fsdp"),
        P(("replica", "fsdp"), None),
    )
    return jax.shard_map(
        per_device,
        mesh=mesh,
        in_specs=placed,
        out_specs=placed,
        check_vma=False,
    )
```

time: 102 us -> 31.7 us (0.31)
  waiting for transfers between devices: 67.3 us -> 0 us
  Pallas kernels: 0 us -> 31 us
  between operations: 14.1 us -> 0.64 us
  blocking collectives: 9.78 us -> 0 us
  other arithmetic: 4.31 us -> 0 us
  local copies, waits for them, and re-layouts: 3.7 us -> 0 us
  matrix products: 1.99 us -> 0 us
    reduce_scatter x1 -> x0, waiting for transfers between devices: 39.2 us -> none  [per_device(): lax.psum_scatter(pseudo.astype(jnp.float32), 'replica', scatter_dimension...]
    pallas_call x0 -> x2, Pallas kernels: none -> 31 us  [the longest x1 29.3 us: per_device(): pl.pallas_call(functools.partial(kernel, n_r, n_f, chunks, fold), out_sha...]
    all_gather x1 -> x0, waiting for transfers between devices: 28.1 us -> none  [per_device(): lax.all_gather(blended, 'fsdp', axis=1, tiled=True)]
    all_gather x1 -> x0, blocking collectives: 9.78 us -> none  [per_device(): anchor_out = lax.all_gather(new_slice, 'replica', axis=0, tiled=True)]
    unnamed x8 -> x0, local copies, waits for them, and re-layouts: 3.7 us -> none
    convert_element_type x3 -> x0, other arithmetic: 2.8 us -> none  [the longest x1 1.19 us: per_device(): pseudo = (anchor - own_weight.astype(jnp.float32)).astype(jnp.bfloat16)]
    dot_general x1 -> x0, matrix products: 1.99 us -> none  [per_device(): jnp.dot(tokens, lax.all_gather(blended, 'fsdp', axis=1, tiled=True), pref...]
    sub x1 -> x0, other arithmetic: 1.52 us -> none  [per_device(): anchor_slice - outer_rate * (average + decay_rate * momentum_out)]
  transfers between devices with their start and end apart: 2 -> 0, of which waited for: 2 -> 0; matrix products, arithmetic and copies ran while one was open for 0% -> 0% of each run, Pallas kernels for 0% -> 0%
where the time goes in v3:
time: 31.7 us; the launch traced here: 31.6 us
  Pallas kernels  31 us (98%)
  between operations  0.64 us (2%)
    pallas_call x1, Pallas kernels, per_device(): pl.pallas_call(functools.partial(kernel, n_r, n_f, chunks, fold), out_sha...  29.3 us
    pallas_call x1, Pallas kernels, per_device(): pl.pallas_call(write_out, out_shape=[jax.ShapeDtypeStruct(x.shape, x.dtyp...  1.64 us

profile of v3, /device:TPU:0, one launch (start us, length us, event | category | flops | bytes accessed | tf_op | source)
XLA Modules:
  0.0 31.6 jit_solution(7025288360393047352)
XLA Ops:
  0.6 29.3 %shard_map.75 = (bf16[1,64,2048]{2,1,0:T(8,128)(2,1)S(1)}, f32[64,2048]{1,0:T(8,128)S(1)}, f32[8,2048]{1,0:T(8,128)S(1)}, bf16[128,8192]{1,0:T(8,128)(2,1)S(1)}) custom-call(bf16[1,64,2048]{2,1,0:T(8,128)(2,1)} %lw_hbm.1, f32[64,2048]{1,0:T(8,128)} %anchor_hbm.1, f32[8,2048]{1,0:T(8,128)} %mom_hbm.1, bf16[64,128]{1,0:T(8,128)(2,1)} %bitcast.1), custom_call_target="tpu_custom_call" | custom-call | flops 134217728 | bytes 3670016 | tf_op jit(solution)/shard_map/pallas_call | solution.py:285
  30.0 1.6 %shard_map.76 = (bf16[1,64,2048]{2,1,0:T(8,128)(2,1)}, f32[64,2048]{1,0:T(8,128)}, f32[8,2048]{1,0:T(8,128)}, bf16[128,8192]{1,0:T(8,128)(2,1)}) custom-call(bf16[1,64,2048]{2,1,0:T(8,128)(2,1)S(1)} %get-tuple-element.8.refs_0_, f32[64,2048]{1,0:T(8,128)S(1)} %get-tuple-element.9.refs_1_, f32[8,2048]{1,0:T(8,128)S(1)} %get-tuple-element.10.refs_2_, ...), custom_call_target="tpu_custom_call" | custom-call | tf_op jit(solution)/shard_map/pallas_call | solution.py:327

commit v4 on v3

--- a/solution.py
+++ b/solution.py
@@ -49,6 +49,18 @@
 
         lax.fori_loop(1, n_r, step, 0)
 
+    def mate_of(device):
+        return device + 1 - 2 * lax.rem(device, 2)
+
+    mate = mate_of(r)
+
+    def each_far(body):
+        def step(i, _):
+            body(lax.rem(r + 2 * i, n_r))
+            return 0
+
+        lax.fori_loop(1, n_r // 2, step, 0)
+
     def each_place(body):
         def step(i, _):
             body(lax.rem(f + i, n_f))
@@ -91,12 +103,12 @@
             device_id_type=MESH,
         )
 
-    def ag_copy(peer, owner):
+    def ag_copy(peer, owner, slot):
         block = aout_ref.at[pl.ds(pl.multiple_of(owner * rows, rows), rows), :]
         return pltpu.make_async_remote_copy(
             src_ref=block,
             dst_ref=block,
-            send_sem=ag_ssem.at[peer],
+            send_sem=ag_ssem.at[slot],
             recv_sem=ag_rsem.at[owner],
             device_id=(peer, f),
             device_id_type=MESH,
@@ -122,15 +134,42 @@
             device_id_type=MESH,
         )
 
-    def d_copy(peer, block, owner):
+    def d_copy(peer, block, owner, slot):
         return pltpu.make_async_remote_copy(
             src_ref=news.at[block, owner],
             dst_ref=news.at[block, owner],
-            send_sem=d_ssem.at[block, peer],
+            send_sem=d_ssem.at[block, slot],
             recv_sem=d_rsem.at[block, owner],
             device_id=(peer, f),
             device_id_type=MESH,
         )
+
+    def send_rows(copy):
+        each_far(lambda far: copy(far, r, far).start())
+        copy(mate, r, mate).start()
+
+    def relay_rows(copy):
+        def step(far):
+            copy(far, far, far).wait_recv()
+            copy(mate, far, mate_of(far)).start()
+
+        each_far(step)
+
+    def await_rows(copy):
+        copy(mate, mate, mate).wait_recv()
+        each_far(lambda far: copy(mate, mate_of(far), mate).wait_recv())
+
+    def rows_sent(copy):
+        copy(mate, r, mate).wait_send()
+
+        def step(far):
+            copy(far, r, far).wait_send()
+            copy(mate, far, mate_of(far)).wait_send()
+
+        each_far(step)
+
+    def rows_of(block):
+        return lambda peer, owner, slot: d_copy(peer, block, owner, slot)
 
     def send_on(c, block):
         @pl.when((block <= f) & (f < n_f - 1))
@@ -175,7 +214,7 @@
         [new[:, k * half : (k + 1) * half] for k in range(fold)], axis=0
     ).astype(jnp.bfloat16)
     each_place(lambda place: n_copy(place, f).start())
-    each_peer(lambda peer: ag_copy(peer, r).start())
+    send_rows(ag_copy)
 
     def forward(k):
         for c in range(chunks):
@@ -189,9 +228,12 @@
     def spread(k):
         def body(block):
             n_copy(block, block).wait_recv()
-            each_peer(lambda peer: d_copy(peer, block, r).start())
+            send_rows(rows_of(block))
 
         at_distance(k, body)
+
+    def relay(k):
+        at_distance(k, lambda block: relay_rows(rows_of(block)))
 
     def multiply(c, block, weight):
         prod_ref[:, pl.ds(pl.multiple_of(block * cols + c * w, w), w)] = lax.dot_general(
@@ -207,10 +249,7 @@
         ).astype(jnp.bfloat16)
 
     def finish(k):
-        at_distance(
-            k,
-            lambda block: each_peer(lambda peer: d_copy(peer, block, peer).wait_recv()),
-        )
+        at_distance(k, lambda block: await_rows(rows_of(block)))
         for c in range(chunks):
             part, start = (c * w) // half, (c * w) % half
 
@@ -225,12 +264,14 @@
 
             at_distance(k, body)
 
-    spread(1)
     if n_f > 2:
         forward(1)
+    spread(1)
+    relay_rows(ag_copy)
     for k in range(2, n_f):
         spread(k)
-    each_peer(lambda peer: ag_copy(peer, peer).wait_recv())
+        relay(k - 1)
+    await_rows(ag_copy)
     for c in range(chunks):
         at = slice(c * w, (c + 1) * w)
         blended = blend(aout_ref[:, at], weights[f, c])
@@ -239,14 +280,13 @@
     for k in range(1, n_f):
         if k + 1 < n_f - 1:
             forward(k + 1)
+        if k == 1:
+            relay(n_f - 1)
         finish(k)
 
-    def sent(peer):
-        rs_copy(peer, r).wait_send()
-        ag_copy(peer, r).wait_send()
-        each_place(lambda place: d_copy(peer, place, r).wait_send())
-
-    each_peer(sent)
+    each_peer(lambda peer: rs_copy(peer, r).wait_send())
+    rows_sent(ag_copy)
+    each_place(lambda place: rows_sent(rows_of(place)))
     each_place(lambda place: n_copy(place, f).wait_send())
     for c in range(chunks):
         for k in range(n_f):

time: 31.7 us -> 31.1 us (0.981)
  Pallas kernels: 31 us -> 30.3 us
    pallas_call x1, Pallas kernels: 29.3 us -> 28.7 us  [per_device(): pl.pallas_call(functools.partial(kernel, n_r, n_f, chunks, fold), out_sha...]
where the time goes in v4:
time: 31.1 us; the launch traced here: 31 us
  Pallas kernels  30.3 us (97%)
  between operations  0.64 us (2%)
    pallas_call x1, Pallas kernels, per_device(): pl.pallas_call(functools.partial(kernel, n_r, n_f, chunks, fold), out_sha...  28.7 us
    pallas_call x1, Pallas kernels, per_device(): pl.pallas_call(write_out, out_shape=[jax.ShapeDtypeStruct(x.shape, x.dtyp...  1.64 us

profile of v4, /device:TPU:0, one launch (start us, length us, event | category | flops | bytes accessed | tf_op | source)
XLA Modules:
  0.0 31.0 jit_solution(12169866009792698649)
XLA Ops:
  0.6 28.7 %shard_map.75 = (bf16[1,64,2048]{2,1,0:T(8,128)(2,1)S(1)}, f32[64,2048]{1,0:T(8,128)S(1)}, f32[8,2048]{1,0:T(8,128)S(1)}, bf16[128,8192]{1,0:T(8,128)(2,1)S(1)}) custom-call(bf16[1,64,2048]{2,1,0:T(8,128)(2,1)} %lw_hbm.1, f32[64,2048]{1,0:T(8,128)} %anchor_hbm.1, f32[8,2048]{1,0:T(8,128)} %mom_hbm.1, bf16[64,128]{1,0:T(8,128)(2,1)} %bitcast.1), custom_call_target="tpu_custom_call" | custom-call | flops 134217728 | bytes 3670016 | tf_op jit(solution)/shard_map/pallas_call | solution.py:325
  29.3 1.6 %shard_map.76 = (bf16[1,64,2048]{2,1,0:T(8,128)(2,1)}, f32[64,2048]{1,0:T(8,128)}, f32[8,2048]{1,0:T(8,128)}, bf16[128,8192]{1,0:T(8,128)(2,1)}) custom-call(bf16[1,64,2048]{2,1,0:T(8,128)(2,1)S(1)} %get-tuple-element.8.refs_0_, f32[64,2048]{1,0:T(8,128)S(1)} %get-tuple-element.9.refs_1_, f32[8,2048]{1,0:T(8,128)S(1)} %get-tuple-element.10.refs_2_, ...), custom_call_target="tpu_custom_call" | custom-call | tf_op jit(solution)/shard_map/pallas_call | solution.py:367

commit v5 on v4

--- a/solution.py
+++ b/solution.py
@@ -271,6 +271,8 @@
     for k in range(2, n_f):
         spread(k)
         relay(k - 1)
+    if n_f > 3:
+        forward(2)
     await_rows(ag_copy)
     for c in range(chunks):
         at = slice(c * w, (c + 1) * w)
@@ -278,7 +280,7 @@
         blend_ref[0, :, at] = blended
         multiply(c, f, blended)
     for k in range(1, n_f):
-        if k + 1 < n_f - 1:
+        if 1 < k < n_f - 2:
             forward(k + 1)
         if k == 1:
             relay(n_f - 1)

time: 31.1 us -> 30.7 us (0.987)
  Pallas kernels: 30.3 us -> 29.9 us
    pallas_call x1, Pallas kernels: 28.7 us -> 28.3 us  [per_device(): pl.pallas_call(functools.partial(kernel, n_r, n_f, chunks, fold), out_sha...]
where the time goes in v5:
time: 30.7 us; the launch traced here: 30.6 us
  Pallas kernels  29.9 us (97%)
  between operations  0.64 us (2%)
    pallas_call x1, Pallas kernels, per_device(): pl.pallas_call(functools.partial(kernel, n_r, n_f, chunks, fold), out_sha...  28.3 us
    pallas_call x1, Pallas kernels, per_device(): pl.pallas_call(write_out, out_shape=[jax.ShapeDtypeStruct(x.shape, x.dtyp...  1.64 us

profile of v5, /device:TPU:0, one launch (start us, length us, event | category | flops | bytes accessed | tf_op | source)
XLA Modules:
  0.0 30.6 jit_solution(18308321931790067381)
XLA Ops:
  0.6 28.3 %shard_map.75 = (bf16[1,64,2048]{2,1,0:T(8,128)(2,1)S(1)}, f32[64,2048]{1,0:T(8,128)S(1)}, f32[8,2048]{1,0:T(8,128)S(1)}, bf16[128,8192]{1,0:T(8,128)(2,1)S(1)}) custom-call(bf16[1,64,2048]{2,1,0:T(8,128)(2,1)} %lw_hbm.1, f32[64,2048]{1,0:T(8,128)} %anchor_hbm.1, f32[8,2048]{1,0:T(8,128)} %mom_hbm.1, bf16[64,128]{1,0:T(8,128)(2,1)} %bitcast.1), custom_call_target="tpu_custom_call" | custom-call | flops 134217728 | bytes 3670016 | tf_op jit(solution)/shard_map/pallas_call | solution.py:327
  28.9 1.6 %shard_map.76 = (bf16[1,64,2048]{2,1,0:T(8,128)(2,1)}, f32[64,2048]{1,0:T(8,128)}, f32[8,2048]{1,0:T(8,128)}, bf16[128,8192]{1,0:T(8,128)(2,1)}) custom-call(bf16[1,64,2048]{2,1,0:T(8,128)(2,1)S(1)} %get-tuple-element.8.refs_0_, f32[64,2048]{1,0:T(8,128)S(1)} %get-tuple-element.9.refs_1_, f32[8,2048]{1,0:T(8,128)S(1)} %get-tuple-element.10.refs_2_, ...), custom_call_target="tpu_custom_call" | custom-call | tf_op jit(solution)/shard_map/pallas_call | solution.py:369
